TPU v7x, 512 devices: a whole 4x8x8 slice. The times are simulated.
512 devices in a mesh: node: 16 (over z, core), rep: 32 (over x, y).
Axes of the slice: x: 4, y: 8, z: 8, core: 2. Of those that a mesh axis runs over, the one named last changes fastest.
Arguments:
- grads: bfloat16 [16, 32, 4096, 128], P('node', 'rep'), may hold values from -16 to 16, as said below
- feedback: bfloat16 [16, 32, 4096, 128], P('node', 'rep'), may hold values from -0.5 to 0.5, as said below
- master: float32 [4096, 128], P(('node', 'rep')), may hold values from -6 to 6
- moment: float32 [4096, 128], P(('node', 'rep')), may hold values from -0.75 to 0.75
- second: float32 [4096, 128], P(('node', 'rep')), may hold values from 0.0001 to 0.01
Outputs:
- fresh_feedback: bfloat16 [16, 32, 4096, 128], P('node', 'rep')
- mean_grad: float32 [4096, 128], P(('node', 'rep'))
- new_master: float32 [4096, 128], P(('node', 'rep'))
- new_moment: float32 [4096, 128], P(('node', 'rep'))
- new_second: float32 [4096, 128], P(('node', 'rep'))
- weights: bfloat16 [4096, 128], replicated
Inputs may be any that keep to these rules, and one draw needn't show every extreme that they name: `grads`: every entry is a multiple of 1/16. `feedback`: every entry is a multiple of 1/128.
All inputs are finite; a program needn't handle non-finite values.
Results may differ from a plain program's by a relative error of at most 0.001.
Values may be sent and summed in bfloat16 or wider, within the bound.
A program may use at most 64 MiB of HBM per device.

v0:
```python
import jax
import jax.numpy as jnp
import numpy as np
from jax import lax
from jax.sharding import PartitionSpec as P

POWERS = np.power(2.0, np.arange(-24, 25))


def encode(values, levels, bound):
    largest = jnp.max(jnp.abs(values), axis=-1, keepdims=True)
    table = jnp.asarray(POWERS, dtype=jnp.float32)
    picked = jnp.where(table >= largest, table, table[-1])
    scale = jnp.min(picked, axis=-1, keepdims=True).astype(jnp.bfloat16)
    code = jnp.clip(
        jnp.floor(values / scale.astype(jnp.float32) * levels + 0.5), -bound, bound
    ).astype(jnp.bfloat16)
    return (code, scale)


def decode(code, scale, levels):
    return scale.astype(jnp.float32) * code.astype(jnp.float32) / levels


def local(grads, feedback, master, moment, second):
    code_three, scale_three = encode(master, 128.0, 127.0)
    local_weights = decode(code_three, scale_three, 128.0).astype(jnp.bfloat16)
    weights = lax.all_gather(local_weights, ("node", "rep"), axis=0, tiled=True)
    summed = grads[0, 0].astype(jnp.float32) + feedback[0, 0].astype(jnp.float32)
    code_one, scale_one = encode(summed, 8.0, 7.0)
    decoded = decode(code_one, scale_one, 8.0)
    fresh_feedback = (summed - decoded).astype(jnp.bfloat16)[None, None]
    rows, width = summed.shape
    nodes = lax.axis_size("node")
    replicas = lax.axis_size("rep")
    group_rows = rows // nodes
    sent_one = decoded.astype(jnp.bfloat16).reshape(nodes, group_rows, width)
    got_one = lax.all_to_all(sent_one, "node", split_axis=0, concat_axis=0, tiled=True)
    partial_value = jnp.sum(got_one.astype(jnp.float32), axis=0)
    code_two, scale_two = encode(partial_value, 8.0, 7.0)
    shard_rows = group_rows // replicas
    sent_two = (
        decode(code_two, scale_two, 8.0).astype(jnp.bfloat16).reshape(replicas, shard_rows, width)
    )
    got_two = lax.all_to_all(sent_two, "rep", split_axis=0, concat_axis=0, tiled=True)
    mean_grad = jnp.sum(got_two.astype(jnp.float32), axis=0) / (nodes * replicas)
    new_moment = 0.9 * moment + 0.1 * mean_grad
    new_second = 0.95 * second + 0.05 * mean_grad * mean_grad
    update = new_moment / 0.6513216 / (jnp.sqrt(new_second / 0.4012631) + 1e-08)
    new_master = master - 0.01 * (update + 0.1 * master)
    return (fresh_feedback, mean_grad, new_master, new_moment, new_second, weights)


def solution(mesh):
    placed = (
        P("node", "rep", None, None),
        P("node", "rep", None, None),
        P(("node", "rep"), None),
        P(("node", "rep"), None),
        P(("node", "rep"), None),
    )
    return jax.shard_map(
        local,
        mesh=mesh,
        in_specs=placed,
        out_specs=(
            P("node", "rep", None, None),
            P(("node", "rep"), None),
            P(("node", "rep"), None),
            P(("node", "rep"), None),
            P(("node", "rep"), None),
            P(),
        ),
        check_vma=False,
    )
```

profile of v0, /device:TPU:1, one launch (start us, length us, event | category | flops | bytes accessed | tf_op | source)
XLA Modules:
  0.0 184.7 jit_solution(1010851107030844734)
XLA Ops:
  7.2 0.0 copy-start.5
  7.2 2.2 %convert_add_fusion = (f32[1,1,4096,128]{3,2,1,0:T(8,128)S(1)}, f32[4096]{0:T(1024)S(1)}) fusion(bf16[1,1,4096,128]{3,2,1,0:T(8,128)(2,1)} %param.9, bf16[1,1,4096,128]{3,2,1,0:T(8,128)(2,1)} %param.8), kind=kLoop, calls=%fused_computation.6 | loop fusion | flops 2617344 | bytes 4210688 | tf_op jit(solution)/shard_map/add | solution.py:29
  9.3 0.0 copy-done.5
  9.4 0.2 select_reduce_fusion
  9.6 0.9 multiply_convert_fusion
  10.5 0.0 copy-start.2
  10.5 0.0 copy-start.3
  10.5 0.0 copy-start.4
  10.5 0.0 copy-start
  10.5 0.0 copy-start.1
  10.5 40.3 %all_to_all.10 = bf16[16,256,128]{2,1,0:T(8,128)(2,1)S(1)} all-to-all(bf16[16,256,128]{2,1,0:T(8,128)(2,1)S(1)} %multiply_convert_fusion), channel_id=1, replica_groups=mesh['node'=16,'rep'=32] {'node'}, dimensions={0} | all-to-all | bytes 2097152 | tf_op jit(solution)/shard_map/all_to_all | solution.py:38
  50.8 0.1 convert_reduce_fusion
  51.0 0.1 abs_reduce_fusion.1
  51.1 0.1 select_reduce_fusion.1
  51.2 0.1 reshape.91
  51.3 0.8 multiply_convert_fusion.1
  52.0 9.7 %all-to-all-start.1 = ((bf16[32,8,128]{2,1,0:T(8,128)(2,1)}), bf16[32,8,128]{2,1,0:T(8,128)(2,1)S(1)}, u32[]{:S(2)}, u32[]{:S(2)}) async-start(bf16[32,8,128]{2,1,0:T(8,128)(2,1)} %multiply_convert_fusion.1), calls=%async_computation.1 | async-start | bytes 131072 | tf_op jit(solution)/shard_map/all_to_all | solution.py:45
  61.7 0.0 all-gather.2.cloned.1.call-start
  61.8 0.0 copy-done.2
  61.8 0.1 abs_reduce_fusion.2
  61.9 0.2 select_reduce_fusion.2
  62.1 8.8 %all-to-all-done.1 = bf16[32,8,128]{2,1,0:T(8,128)(2,1)S(1)} async-done(((bf16[32,8,128]{2,1,0:T(8,128)(2,1)}), bf16[32,8,128]{2,1,0:T(8,128)(2,1)S(1)}, u32[]{:S(2)}, u32[]{:S(2)}) %all-to-all-start.1) | async-done | bytes 65568 | tf_op jit(solution)/shard_map/all_to_all | solution.py:45
  70.9 0.0 copy-done.3
  70.9 0.0 copy-done.4
  70.9 0.7 multiply_subtract_fusion
  71.6 0.0 all-gather.2.cloned.1.call-update
  71.6 0.0 copy-done
  71.6 0.0 copy-done.1
  71.6 1.8 subtract_convert_fusion
  73.4 102.2 %all-gather.2.cloned.1.call-done = bf16[4096,128]{1,0:T(8,128)(2,1)} async-done(((bf16[8,128]{1,0:T(8,128)(2,1)}), bf16[4096,128]{1,0:T(8,128)(2,1)}) %all-gather.2.cloned.1.call-update) | async-done | bytes 1048592 | tf_op jit(solution)/shard_map/all_gather | solution.py:28
  175.6 2.3 %copy.15 = bf16[4096,128]{1,0:T(8,128)(2,1)} copy(bf16[4096,128]{1,0:T(8,128)(2,1)} %all-gather.2.cloned.1.call-done) | data formatting | bytes 2097152
  (4 shorter events, 0.1 us)
Async XLA Ops:
  7.2 2.2 %copy-start.5 = (f32[49]{0:T(128)S(1)}, f32[49]{0:T(128)}, u32[]{:S(2)}) copy-start(f32[49]{0:T(128)} %constant.54.clone) | copy-start | bytes 592
  10.5 51.3 %copy-start.2 = (f32[8,128]{1,0:T(8,128)S(1)}, f32[8,128]{1,0:T(8,128)}, u32[]{:S(2)}) copy-start(f32[8,128]{1,0:T(8,128)} %param.10) | copy-start | bytes 12292
  10.5 60.4 %copy-start.3 = (f32[8,128]{1,0:T(8,128)S(1)}, f32[8,128]{1,0:T(8,128)}, u32[]{:S(2)}) copy-start(f32[8,128]{1,0:T(8,128)} %param.11) | copy-start | bytes 12292
  10.5 60.4 %copy-start.4 = (f32[8,128]{1,0:T(8,128)S(1)}, f32[8,128]{1,0:T(8,128)}, u32[]{:S(2)}) copy-start(f32[8,128]{1,0:T(8,128)} %param.12) | copy-start | bytes 12292
  10.5 61.1 %copy-start = (bf16[1,1,4096,128]{3,2,1,0:T(8,128)(2,1)S(1)}, bf16[1,1,4096,128]{3,2,1,0:T(8,128)(2,1)}, u32[]{:S(2)}) copy-start(bf16[1,1,4096,128]{3,2,1,0:T(8,128)(2,1)} %param.9) | copy-start | bytes 3145732
  10.5 61.1 %copy-start.1 = (bf16[1,1,4096,128]{3,2,1,0:T(8,128)(2,1)S(1)}, bf16[1,1,4096,128]{3,2,1,0:T(8,128)(2,1)}, u32[]{:S(2)}) copy-start(bf16[1,1,4096,128]{3,2,1,0:T(8,128)(2,1)} %param.8) | copy-start | bytes 3145732
  52.0 18.8 %all-to-all-start.1 = ((bf16[32,8,128]{2,1,0:T(8,128)(2,1)}), bf16[32,8,128]{2,1,0:T(8,128)(2,1)S(1)}, u32[]{:S(2)}, u32[]{:S(2)}) async-start(bf16[32,8,128]{2,1,0:T(8,128)(2,1)} %multiply_convert_fusion.1), calls=%async_computation.1 | async-start | bytes 131072 | tf_op jit(solution)/shard_map/all_to_all | solution.py:45
  61.7 113.9 %all-gather.2.cloned.1.call-start = ((), (), s32[]{:S(2)}) async-start(), calls=%async_computation.2 | async-start | bytes 1050624 | tf_op jit(solution)/shard_map/all_gather | solution.py:28
Sparse Core Ops, SparseCore 0:
  71.7 103.8 all-gather.1
where the time goes:
time: 185 us
  waiting for transfers between devices  111 us (60%)
  blocking collectives  40.3 us (22%)
  between operations  14.2 us (8%)
  starting transfers between devices  9.71 us (5%)
  other arithmetic  7.2 us (4%)
  local copies, waits for them, and re-layouts  2.39 us (1%)
    all_gather x1, waiting for transfers between devices, local(): weights = lax.all_gather(local_weights, ('node', 'rep'), axis=0, tiled=True)  102 us
    all_to_all x1, blocking collectives, local(): lax.all_to_all(sent_one, 'node', split_axis=0, concat_axis=0, tiled=True)  40.3 us
    all_to_all x1, starting transfers between devices, local(): lax.all_to_all(sent_two, 'rep', split_axis=0, concat_axis=0, tiled=True)  9.67 us
    all_to_all x1, waiting for transfers between devices, local(): lax.all_to_all(sent_two, 'rep', split_axis=0, concat_axis=0, tiled=True)  8.76 us
  transfers between devices with their start and end apart: 2, of which 2 were waited for; matrix products, arithmetic and copies ran while one was open for 1% of the time, Pallas kernels for 0%

commit v1 on v0

v1 whole, which is shorter than its diff:
```python
import functools

import jax
import jax.numpy as jnp
from jax import lax
from jax.experimental import pallas as pl
from jax.experimental.pallas import tpu as pltpu
from jax.sharding import PartitionSpec as P

LANES = 128
MESH = pl.DeviceIdType.MESH
ONE_BIT = 1.5 * (1.0 - 2.0**-21)


def power_of(values):
    largest = jnp.max(jnp.abs(values), axis=-1, keepdims=True)
    raised = largest * ONE_BIT
    big = raised * float(2**23)
    return (raised + big) - big


def decoded_of(values, nudge):
    scale = power_of(values)
    magic = scale * float(1.5 * 2**20)
    bound = scale * 0.875
    rounded = ((values + nudge) + magic) - magic
    return jnp.minimum(jnp.maximum(rounded, -bound), bound)


def encode_master(values):
    largest = jnp.max(jnp.abs(values), axis=-1, keepdims=True)
    scale = jnp.full_like(largest, 2.0**24)
    inverse = jnp.full_like(largest, 2.0**-24)
    for k in range(23, -25, -1):
        fits = largest <= 2.0**k
        scale = jnp.where(fits, 2.0**k, scale)
        inverse = jnp.where(fits, 2.0**-k, inverse)
    code = jnp.floor(values * inverse * 128.0 + 0.5)
    code = jnp.minimum(jnp.maximum(code, -127.0), 127.0)
    return scale * code * (1.0 / 128.0)


def exchange(dims, g_hbm, f_hbm, master_ref, ff_ref, w_ref, total_ref,
             gbuf, fbuf, dbuf, sbuf, leaf, pay, out, ebuf, abuf,
             load_sem, sib_s, sib_r, leaf_s, leaf_r, pay_s, pay_r,
             az_s, az_r, ay_s, ay_r, ax_s, ax_r, ac_s, ac_r, two_s, two_r):
    Z, NX, NY, H = dims
    K = Z // 2
    R = NX * NY
    n = lax.axis_index("node")
    r = lax.axis_index("rep")
    z, c = n // 2, n % 2
    x, y = r // NY, r % NY
    oc = 1 - c

    def zoff(off):
        return lax.rem(z + off + Z, Z)

    def dev(off, core):
        return (zoff(off) * 2 + core, r)

    order = [K]
    for k in range(K - 1, 0, -1):
        order += [-k, k]
    order += [0]
    loads = {}
    for i, off in enumerate(order):
        d = zoff(off)
        loads[off] = [
            pltpu.make_async_copy(g_hbm.at[d], gbuf.at[d], load_sem.at[0, i]),
            pltpu.make_async_copy(f_hbm.at[d], fbuf.at[d], load_sem.at[1, i]),
        ]
        for cp in loads[off]:
            cp.start()

    barrier = pltpu.get_barrier_semaphore()
    for off in range(1, Z):
        pl.semaphore_signal(barrier, inc=1, device_id=dev(off, c), device_id_type=MESH)
    for off in (-1, 0, 1):
        pl.semaphore_signal(barrier, inc=1, device_id=dev(off, oc), device_id_type=MESH)

    def greet(i, carry):
        pl.semaphore_signal(barrier, inc=1, device_id=(n, lax.rem(r + i, R)), device_id_type=MESH)
        return carry

    lax.fori_loop(1, R, greet, 0)

    def encode(off):
        d = zoff(off)
        for cp in loads[off]:
            cp.wait()

        def body(i, carry):
            cc, h = i // 2, i % 2
            xv = gbuf[d, cc, h].astype(jnp.float32) + fbuf[d, cc, h].astype(jnp.float32)
            dec = decoded_of(xv, 2.0**-12)
            dbuf[d, cc, h] = dec.astype(jnp.bfloat16)
            ff_ref[d, cc, h] = (xv - dec).astype(jnp.bfloat16)
            return carry

        lax.fori_loop(0, 4, body, 0)

    waits = []

    def remote(src, dst, ssem, rsem, to):
        cp = pltpu.make_async_remote_copy(
            src_ref=src, dst_ref=dst, send_sem=ssem, recv_sem=rsem, device_id=to, device_id_type=MESH
        )
        cp.start()
        waits.append(cp)
        return cp

    w_ref[z, c, x, y] = encode_master(master_ref[...]).astype(jnp.bfloat16)
    encode(K)
    pl.semaphore_wait(barrier, (Z - 1) + 3 + (R - 1))

    def level(dr, h):
        return K if dr == h else K - 1

    def sgn(dr):
        return -1 if dr == 0 else 1

    def send_leaf(dr, h):
        d = zoff(sgn(dr) * level(dr, h))
        for cc in range(2):
            remote(dbuf.at[d, cc, h], leaf.at[dr, h, c], leaf_s.at[dr, h, cc], leaf_r.at[dr, h, c],
                   dev(sgn(dr), cc))

    sib = {}

    def send_sib(off, h=None):
        d = zoff(off)
        if h is None:
            src, dst = dbuf.at[d, oc], sbuf.at[d]
        else:
            src, dst = dbuf.at[d, oc, h], sbuf.at[d, h]
        sib[off] = remote(src, dst, sib_s.at[off + K], sib_r.at[off + K], dev(0, oc))

    sib_seen = set()

    def wait_sib(off):
        if off not in sib_seen:
            sib_seen.add(off)
            sib[off].wait_recv()

    def received(dr, h, k):
        if k + 1 == level(dr, h):
            for src in range(2):
                pltpu.make_async_copy(leaf.at[dr, h, src], leaf.at[dr, h, src], leaf_r.at[dr, h, src]).wait()
            return leaf[dr, h, 0].astype(jnp.float32) + leaf[dr, h, 1].astype(jnp.float32)
        pltpu.make_async_copy(pay.at[dr, h, k], pay.at[dr, h, k], pay_r.at[dr, h, k]).wait()
        return pay[dr, h, k]

    def send_pay(dr, h, k):
        off = sgn(dr) * k
        d = zoff(off)
        wait_sib(off)
        acc = dbuf[d, c, h].astype(jnp.float32) + sbuf[d, h].astype(jnp.float32)
        out[dr, h, k] = acc + received(dr, h, k)
        remote(out.at[dr, h, k], pay.at[dr, h, k - 1], pay_s.at[dr, h, k], pay_r.at[dr, h, k - 1],
               dev(sgn(dr), c))

    send_leaf(0, 0)
    send_leaf(1, 1)
    gz = [remote(w_ref.at[z, c, x, y], w_ref.at[z, c, x, y], az_s.at[off], az_r.at[off], dev(off, c))
          for off in range(1, Z)]
    encode(-(K - 1))
    send_leaf(0, 1)
    send_sib(-(K - 1), 0)
    encode(K - 1)
    send_leaf(1, 0)
    send_sib(K - 1, 1)
    for cp in gz:
        cp.wait_recv()
    gy = [remote(w_ref.at[:, c, x, y], w_ref.at[:, c, x, y], ay_s.at[off], ay_r.at[off],
                 (n, x * NY + lax.rem(y + off, NY))) for off in range(1, NY)]
    for k in range(K - 2, 0, -1):
        encode(-k)
        send_sib(-k)
        encode(k)
        send_sib(k)
    encode(0)
    send_sib(0)

    gx, gc = [], []
    for k in range(K - 1, 0, -1):
        for second in (True, False):
            for dr in range(2):
                h = dr if not second else 1 - dr
                if k < level(dr, h):
                    send_pay(dr, h, k)
        if k == K - 1:
            for cp in gy:
                cp.wait_recv()
            gx = [remote(w_ref.at[:, c, x], w_ref.at[:, c, x], ax_s.at[off], ax_r.at[off],
                         (n, lax.rem(x + off, NX) * NY + y)) for off in range(1, NX)]
            gc.append(remote(w_ref.at[:, c, x], w_ref.at[:, c, x], ac_s.at[0], ac_r.at[0], dev(0, oc)))

    G = R // 2
    wait_sib(0)
    for h in (1, 0):
        part = dbuf[z, c, h].astype(jnp.float32) + sbuf[z, h].astype(jnp.float32)
        part = part + received(0, h, 0) + received(1, h, 0)
        two = decoded_of(part, 2.0**-15)
        ebuf[h * G:(h + 1) * G] = two.reshape(G, 8, LANES).astype(jnp.bfloat16)

        def spread(i, carry):
            @pl.when(i != r)
            def _():
                pltpu.make_async_remote_copy(
                    src_ref=ebuf.at[i], dst_ref=abuf.at[r], send_sem=two_s, recv_sem=two_r,
                    device_id=(n, i), device_id_type=MESH).start()
            return carry

        lax.fori_loop(h * G, (h + 1) * G, spread, 0)

    for off, cp in enumerate(gx, 1):
        cp.wait_recv()
        xs = lax.rem(x - off + NX, NX)
        gc.append(remote(w_ref.at[:, c, xs], w_ref.at[:, c, xs], ac_s.at[off], ac_r.at[off], dev(0, oc)))

    abuf[r] = ebuf[r]
    rest = abuf.at[pl.ds(0, R - 1)]
    pltpu.make_async_copy(rest, rest, two_r).wait()
    total_ref[...] = jnp.sum(abuf[...].astype(jnp.float32), axis=0)
    for cp in gc:
        cp.wait_recv()
    for cp in waits:
        cp.wait_send()
    pltpu.make_async_copy(rest, rest, two_s).wait()


def finish(devices, total_ref, master_ref, moment_ref, second_ref, ff_in, w_in,
           ff_out, mean_ref, master_out, moment_out, second_out, w_out, sem):
    copies = [pltpu.make_async_copy(ff_in.at[i], ff_out.at[i], sem.at[0, i]) for i in range(ff_in.shape[0])]
    copies += [pltpu.make_async_copy(w_in.at[i], w_out.at[i], sem.at[1, i]) for i in range(w_in.shape[0])]
    for cp in copies:
        cp.start()
    mean = total_ref[...] * (1.0 / devices)
    moment = 0.9 * moment_ref[...] + 0.1 * mean
    second = 0.95 * second_ref[...] + 0.05 * mean * mean
    master = master_ref[...]
    update = moment / 0.6513216 / (jnp.sqrt(second / 0.4012631) + 1e-08)
    mean_ref[...] = mean
    moment_out[...] = moment
    second_out[...] = second
    master_out[...] = master - 0.01 * (update + 0.1 * master)
    for cp in copies:
        cp.wait()


def local(grads, feedback, master, moment, second):
    nodes, R = lax.axis_size("node"), lax.axis_size("rep")
    rows = grads.shape[2]
    Z = nodes // 2
    K = Z // 2
    NX = {32: 4, 4: 2}.get(R, 1)
    NY = R // NX
    H = rows // nodes // 2
    bf, f32 = jnp.bfloat16, jnp.float32
    blocks = (Z, 2, 2, H, LANES)
    wshape = (Z, 2, NX, NY, 8, LANES)
    any_, vmem = pl.BlockSpec(memory_space=pl.ANY), pl.BlockSpec(memory_space=pltpu.VMEM)
    dma = pltpu.SemaphoreType.DMA
    ff, weights, total = pl.pallas_call(
        functools.partial(exchange, (Z, NX, NY, H)),
        out_shape=(
            jax.ShapeDtypeStruct(blocks, bf),
            jax.ShapeDtypeStruct(wshape, bf),
            jax.ShapeDtypeStruct((8, LANES), f32),
        ),
        in_specs=[any_, any_, vmem],
        out_specs=(vmem, vmem, vmem),
        scratch_shapes=[
            pltpu.VMEM(blocks, bf),
            pltpu.VMEM(blocks, bf),
            pltpu.VMEM(blocks, bf),
            pltpu.VMEM((Z, 2, H, LANES), bf),
            pltpu.VMEM((2, 2, 2, H, LANES), bf),
            pltpu.VMEM((2, 2, K, H, LANES), f32),
            pltpu.VMEM((2, 2, K, H, LANES), f32),
            pltpu.VMEM((R, 8, LANES), bf),
            pltpu.VMEM((R, 8, LANES), bf),
            dma((2, Z)),
            dma((Z + 1,)), dma((Z + 1,)),
            dma((2, 2, 2)), dma((2, 2, 2)),
            dma((2, 2, K)), dma((2, 2, K)),
            dma((Z,)), dma((Z,)),
            dma((NY,)), dma((NY,)),
            dma((NX,)), dma((NX,)),
            dma((NX,)), dma((NX,)),
            dma, dma,
        ],
        compiler_params=pltpu.CompilerParams(
            collective_id=0, has_side_effects=True, vmem_limit_bytes=32 * 2**20
        ),
        cost_estimate=pl.CostEstimate(flops=20 * rows * LANES, bytes_accessed=10 * rows * LANES, transcendentals=0),
        name="exchange",
    )(grads.reshape(blocks), feedback.reshape(blocks), master)
    small = jax.ShapeDtypeStruct((8, LANES), f32)
    ff, mean, new_master, new_moment, new_second, weights = pl.pallas_call(
        functools.partial(finish, nodes * R),
        out_shape=(jax.ShapeDtypeStruct(blocks, bf), small, small, small, small, jax.ShapeDtypeStruct(wshape, bf)),
        in_specs=[vmem] * 4 + [any_] * 2,
        out_specs=(any_, vmem, vmem, vmem, vmem, any_),
        scratch_shapes=[dma((2, Z))],
        cost_estimate=pl.CostEstimate(flops=20 * 8 * LANES, bytes_accessed=8 * rows * LANES, transcendentals=0),
        name="finish",
    )(total, master, moment, second, ff, weights)
    return (ff.reshape(grads.shape), mean, new_master, new_moment, new_second, weights.reshape(rows, LANES))


def solution(mesh):
    each, shard = P("node", "rep", None, None), P(("node", "rep"), None)
    return jax.shard_map(
        local,
        mesh=mesh,
        in_specs=(each, each, shard, shard, shard),
        out_specs=(each, shard, shard, shard, shard, P()),
        check_vma=False,
    )
```

time: 185 us -> 119 us (0.64)
  the two profiles are of different devices: /device:TPU:1 before, /device:TPU:2 now
where the time goes in v1:
time: 119 us; the launch traced here: 118 us
  Pallas kernels  112 us (94%)
  local copies, waits for them, and re-layouts  5.71 us (5%)
    pallas_call x1, Pallas kernels, local(): pl.pallas_call(functools.partial(finish, nodes * R), out_shape=(jax.Shape...  66.1 us
    pallas_call x1, Pallas kernels, local(): pl.pallas_call(functools.partial(exchange, (Z, NX, NY, H)), out_shape=(ja...  45.9 us
    unnamed x12, local copies, waits for them, and re-layouts  5.71 us

profile of v1, /device:TPU:2, one launch (start us, length us, event | category | flops | bytes accessed | tf_op | source)
XLA Modules:
  0.0 118.4 jit_solution(16552009304552134706)
XLA Ops:
  0.6 0.0 copy-start
  0.6 1.2 %copy-done = bf16[1,1,4096,128]{3,2,1,0:T(8,128)(2,1)S(1)} copy-done((bf16[1,1,4096,128]{3,2,1,0:T(8,128)(2,1)S(1)}, bf16[1,1,4096,128]{3,2,1,0:T(8,128)(2,1)}, u32[]{:S(2)}) %copy-start) | copy-done | bytes 1048600
  1.9 0.0 copy-start.1
  1.9 1.2 %copy-done.1 = bf16[1,1,4096,128]{3,2,1,0:T(8,128)(2,1)S(1)} copy-done((bf16[1,1,4096,128]{3,2,1,0:T(8,128)(2,1)S(1)}, bf16[1,1,4096,128]{3,2,1,0:T(8,128)(2,1)}, u32[]{:S(2)}) %copy-start.1) | copy-done | bytes 1048600
  3.1 0.0 copy-start.4
  3.1 0.7 copy-done.4
  3.8 45.9 %exchange.1 = (bf16[8,2,2,128,128]{4,3,2,1,0:T(8,128)(2,1)S(1)}, bf16[8,2,4,8,8,128]{5,4,3,2,1,0:T(8,128)(2,1)S(1)}, f32[8,128]{1,0:T(8,128)S(1)}) custom-call(bf16[8,2,2,128,128]{4,3,2,1,0:T(8,128)(2,1)S(1)} %bitcast.4, bf16[8,2,2,128,128]{4,3,2,1,0:T(8,128)(2,1)S(1)} %bitcast.5, f32[8,128]{1,0:T(8,128)S(1)} %copy-done.4), custom_call_target="tpu_custom_call" | custom-call | flops 10485760 | bytes 5242880 | tf_op jit(solution)/shard_map/exchange/pallas_call | solution.py:265
  49.7 0.0 copy-start.2
  49.7 1.0 copy-done.2
  50.6 0.0 copy-start.3
  50.6 1.0 copy-done.3
  51.7 0.0 copy-start.5
  51.7 0.6 copy-done.5
  52.3 66.1 %finish.1 = (bf16[8,2,2,128,128]{4,3,2,1,0:T(8,128)(2,1)}, f32[8,128]{1,0:T(8,128)}, f32[8,128]{1,0:T(8,128)}, f32[8,128]{1,0:T(8,128)}, f32[8,128]{1,0:T(8,128)}, /*index=5*/bf16[8,2,4,8,8,128]{5,4,3,2,1,0:T(8,128)(2,1)}) custom-call(f32[8,128]{1,0:T(8,128)} %copy-done.5, f32[8,128]{1,0:T(8,128)} %master_ref.3, f32[8,128]{1,0:T(8,128)} %moment_ref.1, ...), custom_call_target="tpu_custom_call" | custom-call | flops 20480 | bytes 4194304 | tf_op jit(solution)/shard_map/finish/pallas_call | solution.py:301
Async XLA Ops:
  0.6 1.2 %copy-start = (bf16[1,1,4096,128]{3,2,1,0:T(8,128)(2,1)S(1)}, bf16[1,1,4096,128]{3,2,1,0:T(8,128)(2,1)}, u32[]{:S(2)}) copy-start(bf16[1,1,4096,128]{3,2,1,0:T(8,128)(2,1)} %param.5) | copy-start | bytes 3145732
  1.9 1.2 %copy-start.1 = (bf16[1,1,4096,128]{3,2,1,0:T(8,128)(2,1)S(1)}, bf16[1,1,4096,128]{3,2,1,0:T(8,128)(2,1)}, u32[]{:S(2)}) copy-start(bf16[1,1,4096,128]{3,2,1,0:T(8,128)(2,1)} %param.6) | copy-start | bytes 3145732
  3.1 0.7 copy-start.4
  49.7 1.0 copy-start.2
  50.6 1.0 copy-start.3
  51.7 0.6 copy-start.5

commit v2 on v1

--- a/solution.py
+++ b/solution.py
@@ -40,9 +40,9 @@
     return scale * code * (1.0 / 128.0)
 
 
-def exchange(dims, g_hbm, f_hbm, master_ref, ff_ref, w_ref, total_ref,
-             gbuf, fbuf, dbuf, sbuf, leaf, pay, out, ebuf, abuf,
-             load_sem, sib_s, sib_r, leaf_s, leaf_r, pay_s, pay_r,
+def exchange(dims, g_hbm, f_hbm, master_hbm, moment_hbm, second_hbm, ff_ref, w_ref, small_ref,
+             gbuf, fbuf, dbuf, sbuf, leaf, pay, out, ebuf, abuf, state,
+             state_sem, load_sem, sib_s, sib_r, leaf_s, leaf_r, pay_s, pay_r,
              az_s, az_r, ay_s, ay_r, ax_s, ax_r, ac_s, ac_r, two_s, two_r):
     Z, NX, NY, H = dims
     K = Z // 2
@@ -59,6 +59,10 @@
     def dev(off, core):
         return (zoff(off) * 2 + core, r)
 
+    states = [pltpu.make_async_copy(ref, state.at[i], state_sem.at[i])
+              for i, ref in enumerate((master_hbm, moment_hbm, second_hbm))]
+    for cp in states:
+        cp.start()
     order = [K]
     for k in range(K - 1, 0, -1):
         order += [-k, k]
@@ -110,7 +114,9 @@
         waits.append(cp)
         return cp
 
-    w_ref[z, c, x, y] = encode_master(master_ref[...]).astype(jnp.bfloat16)
+    for cp in states:
+        cp.wait()
+    w_ref[z, c, x, y] = encode_master(state[0]).astype(jnp.bfloat16)
     encode(K)
     pl.semaphore_wait(barrier, (Z - 1) + 3 + (R - 1))
 
@@ -222,7 +228,15 @@
     abuf[r] = ebuf[r]
     rest = abuf.at[pl.ds(0, R - 1)]
     pltpu.make_async_copy(rest, rest, two_r).wait()
-    total_ref[...] = jnp.sum(abuf[...].astype(jnp.float32), axis=0)
+    mean = jnp.sum(abuf[...].astype(jnp.float32), axis=0) * (1.0 / (2 * Z * R))
+    master = state[0]
+    moment = 0.9 * state[1] + 0.1 * mean
+    second = 0.95 * state[2] + 0.05 * mean * mean
+    update = moment / 0.6513216 / (jnp.sqrt(second / 0.4012631) + 1e-08)
+    small_ref[0] = mean
+    small_ref[1] = master - 0.01 * (update + 0.1 * master)
+    small_ref[2] = moment
+    small_ref[3] = second
     for cp in gc:
         cp.wait_recv()
     for cp in waits:
@@ -230,21 +244,12 @@
     pltpu.make_async_copy(rest, rest, two_s).wait()
 
 
-def finish(devices, total_ref, master_ref, moment_ref, second_ref, ff_in, w_in,
-           ff_out, mean_ref, master_out, moment_out, second_out, w_out, sem):
-    copies = [pltpu.make_async_copy(ff_in.at[i], ff_out.at[i], sem.at[0, i]) for i in range(ff_in.shape[0])]
-    copies += [pltpu.make_async_copy(w_in.at[i], w_out.at[i], sem.at[1, i]) for i in range(w_in.shape[0])]
+def finish(small_ref, ff_in, w_in, ff_out, mean_out, master_out, moment_out, second_out, w_out, sem):
+    copies = [pltpu.make_async_copy(ff_in, ff_out, sem.at[4]), pltpu.make_async_copy(w_in, w_out, sem.at[5])]
+    copies += [pltpu.make_async_copy(small_ref.at[i], out, sem.at[i])
+               for i, out in enumerate((mean_out, master_out, moment_out, second_out))]
     for cp in copies:
         cp.start()
-    mean = total_ref[...] * (1.0 / devices)
-    moment = 0.9 * moment_ref[...] + 0.1 * mean
-    second = 0.95 * second_ref[...] + 0.05 * mean * mean
-    master = master_ref[...]
-    update = moment / 0.6513216 / (jnp.sqrt(second / 0.4012631) + 1e-08)
-    mean_ref[...] = mean
-    moment_out[...] = moment
-    second_out[...] = second
-    master_out[...] = master - 0.01 * (update + 0.1 * master)
     for cp in copies:
         cp.wait()
 
@@ -260,16 +265,16 @@
     bf, f32 = jnp.bfloat16, jnp.float32
     blocks = (Z, 2, 2, H, LANES)
     wshape = (Z, 2, NX, NY, 8, LANES)
-    any_, vmem = pl.BlockSpec(memory_space=pl.ANY), pl.BlockSpec(memory_space=pltpu.VMEM)
+    hbm, vmem = pl.BlockSpec(memory_space=pltpu.HBM), pl.BlockSpec(memory_space=pltpu.VMEM)
     dma = pltpu.SemaphoreType.DMA
-    ff, weights, total = pl.pallas_call(
+    ff, weights, small = pl.pallas_call(
         functools.partial(exchange, (Z, NX, NY, H)),
         out_shape=(
             jax.ShapeDtypeStruct(blocks, bf),
             jax.ShapeDtypeStruct(wshape, bf),
-            jax.ShapeDtypeStruct((8, LANES), f32),
+            jax.ShapeDtypeStruct((4, 8, LANES), f32),
         ),
-        in_specs=[any_, any_, vmem],
+        in_specs=[hbm] * 5,
         out_specs=(vmem, vmem, vmem),
         scratch_shapes=[
             pltpu.VMEM(blocks, bf),
@@ -281,6 +286,8 @@
             pltpu.VMEM((2, 2, K, H, LANES), f32),
             pltpu.VMEM((R, 8, LANES), bf),
             pltpu.VMEM((R, 8, LANES), bf),
+            pltpu.VMEM((3, 8, LANES), f32),
+            dma((3,)),
             dma((2, Z)),
             dma((Z + 1,)), dma((Z + 1,)),
             dma((2, 2, 2)), dma((2, 2, 2)),
@@ -296,17 +303,18 @@
         ),
         cost_estimate=pl.CostEstimate(flops=20 * rows * LANES, bytes_accessed=10 * rows * LANES, transcendentals=0),
         name="exchange",
-    )(grads.reshape(blocks), feedback.reshape(blocks), master)
-    small = jax.ShapeDtypeStruct((8, LANES), f32)
+    )(grads.reshape(blocks), feedback.reshape(blocks), master, moment, second)
+    shard = jax.ShapeDtypeStruct((8, LANES), f32)
     ff, mean, new_master, new_moment, new_second, weights = pl.pallas_call(
-        functools.partial(finish, nodes * R),
-        out_shape=(jax.ShapeDtypeStruct(blocks, bf), small, small, small, small, jax.ShapeDtypeStruct(wshape, bf)),
-        in_specs=[vmem] * 4 + [any_] * 2,
-        out_specs=(any_, vmem, vmem, vmem, vmem, any_),
-        scratch_shapes=[dma((2, Z))],
-        cost_estimate=pl.CostEstimate(flops=20 * 8 * LANES, bytes_accessed=8 * rows * LANES, transcendentals=0),
+        finish,
+        out_shape=(jax.ShapeDtypeStruct(blocks, bf), shard, shard, shard, shard, jax.ShapeDtypeStruct(wshape, bf)),
+        in_specs=[vmem] * 3,
+        out_specs=(hbm,) * 6,
+        scratch_shapes=[dma((6,))],
+        compiler_params=pltpu.CompilerParams(vmem_limit_bytes=8 * 2**20),
+        cost_estimate=pl.CostEstimate(flops=0, bytes_accessed=8 * rows * LANES, transcendentals=0),
         name="finish",
-    )(total, master, moment, second, ff, weights)
+    )(small, ff, weights)
     return (ff.reshape(grads.shape), mean, new_master, new_moment, new_second, weights.reshape(rows, LANES))
 
 

time: 119 us -> 52.8 us (0.44)
  Pallas kernels: 112 us -> 47.3 us
  local copies, waits for them, and re-layouts: 5.71 us -> 4.5 us
    pallas_call x1, Pallas kernels: 66.1 us -> 1.38 us  [local(): pl.pallas_call(finish, out_shape=(jax.ShapeDtypeStruct(blocks, bf), shard...]
    unnamed x12 -> x10, local copies, waits for them, and re-layouts: 5.71 us -> 4.5 us
where the time goes in v2:
time: 52.8 us; the launch traced here: 52.5 us
  Pallas kernels  47.3 us (90%)
  local copies, waits for them, and re-layouts  4.5 us (9%)
  between operations  0.65 us (1%)
    pallas_call x1, Pallas kernels, local(): pl.pallas_call(functools.partial(exchange, (Z, NX, NY, H)), out_shape=(ja...  45.9 us
    unnamed x10, local copies, waits for them, and re-layouts  4.5 us
    pallas_call x1, Pallas kernels, local(): pl.pallas_call(finish, out_shape=(jax.ShapeDtypeStruct(blocks, bf), shard...  1.38 us

profile of v2, /device:TPU:2, one launch (start us, length us, event | category | flops | bytes accessed | tf_op | source)
XLA Modules:
  0.0 52.5 jit_solution(4780945534735134359)
XLA Ops:
  0.6 0.0 copy-start
  0.6 1.2 %copy-done = bf16[1,1,4096,128]{3,2,1,0:T(8,128)(2,1)S(1)} copy-done((bf16[1,1,4096,128]{3,2,1,0:T(8,128)(2,1)S(1)}, bf16[1,1,4096,128]{3,2,1,0:T(8,128)(2,1)}, u32[]{:S(2)}) %copy-start) | copy-done | bytes 1048600
  1.9 0.0 copy-start.1
  1.9 1.2 %copy-done.1 = bf16[1,1,4096,128]{3,2,1,0:T(8,128)(2,1)S(1)} copy-done((bf16[1,1,4096,128]{3,2,1,0:T(8,128)(2,1)S(1)}, bf16[1,1,4096,128]{3,2,1,0:T(8,128)(2,1)}, u32[]{:S(2)}) %copy-start.1) | copy-done | bytes 1048600
  3.1 0.0 copy-start.2
  3.1 0.7 %copy-done.2 = f32[8,128]{1,0:T(8,128)S(1)} copy-done((f32[8,128]{1,0:T(8,128)S(1)}, f32[8,128]{1,0:T(8,128)}, u32[]{:S(2)}) %copy-start.2) | copy-done | bytes 4120
  3.8 0.0 copy-start.3
  3.8 0.7 %copy-done.3 = f32[8,128]{1,0:T(8,128)S(1)} copy-done((f32[8,128]{1,0:T(8,128)S(1)}, f32[8,128]{1,0:T(8,128)}, u32[]{:S(2)}) %copy-start.3) | copy-done | bytes 4120
  4.5 0.0 copy-start.4
  4.5 0.7 %copy-done.4 = f32[8,128]{1,0:T(8,128)S(1)} copy-done((f32[8,128]{1,0:T(8,128)S(1)}, f32[8,128]{1,0:T(8,128)}, u32[]{:S(2)}) %copy-start.4) | copy-done | bytes 4120
  5.1 45.9 %exchange.1 = (bf16[8,2,2,128,128]{4,3,2,1,0:T(8,128)(2,1)S(1)}, bf16[8,2,4,8,8,128]{5,4,3,2,1,0:T(8,128)(2,1)S(1)}, f32[4,8,128]{2,1,0:T(8,128)S(1)}) custom-call(bf16[8,2,2,128,128]{4,3,2,1,0:T(8,128)(2,1)S(1)} %bitcast.4, bf16[8,2,2,128,128]{4,3,2,1,0:T(8,128)(2,1)S(1)} %bitcast.5, f32[8,128]{1,0:T(8,128)S(1)} %copy-done.2, f32[8,128]{1,0:T(8,128)S(1)} %copy-done.3, ...), custom_call_target="tpu_custom_call" | custom-call | flops 10485760 | bytes 5242880 | tf_op jit(solution)/shard_map/exchange/pallas_call | solution.py:270
  51.1 1.4 %finish.1 = (bf16[8,2,2,128,128]{4,3,2,1,0:T(8,128)(2,1)}, f32[8,128]{1,0:T(8,128)}, f32[8,128]{1,0:T(8,128)}, f32[8,128]{1,0:T(8,128)}, f32[8,128]{1,0:T(8,128)}, /*index=5*/bf16[8,2,4,8,8,128]{5,4,3,2,1,0:T(8,128)(2,1)}) custom-call(f32[4,8,128]{2,1,0:T(8,128)S(1)} %get-tuple-element.15.small_ref, ...), custom_call_target="tpu_custom_call" | custom-call | bytes 4194304 | tf_op jit(solution)/shard_map/finish/pallas_call | solution.py:308
Async XLA Ops:
  0.6 1.2 %copy-start = (bf16[1,1,4096,128]{3,2,1,0:T(8,128)(2,1)S(1)}, bf16[1,1,4096,128]{3,2,1,0:T(8,128)(2,1)}, u32[]{:S(2)}) copy-start(bf16[1,1,4096,128]{3,2,1,0:T(8,128)(2,1)} %param.5) | copy-start | bytes 3145732
  1.9 1.2 %copy-start.1 = (bf16[1,1,4096,128]{3,2,1,0:T(8,128)(2,1)S(1)}, bf16[1,1,4096,128]{3,2,1,0:T(8,128)(2,1)}, u32[]{:S(2)}) copy-start(bf16[1,1,4096,128]{3,2,1,0:T(8,128)(2,1)} %param.6) | copy-start | bytes 3145732
  3.1 0.7 %copy-start.2 = (f32[8,128]{1,0:T(8,128)S(1)}, f32[8,128]{1,0:T(8,128)}, u32[]{:S(2)}) copy-start(f32[8,128]{1,0:T(8,128)} %master_hbm.1) | copy-start | bytes 12292
  3.8 0.7 %copy-start.3 = (f32[8,128]{1,0:T(8,128)S(1)}, f32[8,128]{1,0:T(8,128)}, u32[]{:S(2)}) copy-start(f32[8,128]{1,0:T(8,128)} %moment_hbm.1) | copy-start | bytes 12292
  4.5 0.7 %copy-start.4 = (f32[8,128]{1,0:T(8,128)S(1)}, f32[8,128]{1,0:T(8,128)}, u32[]{:S(2)}) copy-start(f32[8,128]{1,0:T(8,128)} %second_hbm.1) | copy-start | bytes 12292

commit v3 on v1

v3 whole, which is shorter than its diff:
```python
import functools

import jax
import jax.numpy as jnp
from jax import lax
from jax.experimental import pallas as pl
from jax.experimental.pallas import tpu as pltpu
from jax.sharding import PartitionSpec as P

LANES = 128
MESH = pl.DeviceIdType.MESH
ONE_BIT = 1.5 * (1.0 - 2.0**-21)


def power_of(values):
    largest = jnp.max(jnp.abs(values), axis=-1, keepdims=True)
    raised = largest * ONE_BIT
    big = raised * float(2**23)
    return (raised + big) - big


def decoded_of(values, nudge):
    scale = power_of(values)
    magic = scale * float(1.5 * 2**20)
    bound = scale * 0.875
    rounded = ((values + nudge) + magic) - magic
    return jnp.minimum(jnp.maximum(rounded, -bound), bound)


def encode_master(values):
    largest = jnp.max(jnp.abs(values), axis=-1, keepdims=True)
    scale = jnp.full_like(largest, 2.0**24)
    inverse = jnp.full_like(largest, 2.0**-24)
    for k in range(23, -25, -1):
        fits = largest <= 2.0**k
        scale = jnp.where(fits, 2.0**k, scale)
        inverse = jnp.where(fits, 2.0**-k, inverse)
    code = jnp.floor(values * inverse * 128.0 + 0.5)
    code = jnp.minimum(jnp.maximum(code, -127.0), 127.0)
    return scale * code * (1.0 / 128.0)


def exchange(dims, g_hbm, f_hbm, master_hbm, ff_ref, w_ref, total_ref,
             gbuf, fbuf, dbuf, sbuf, leaf, pay, out, ebuf, abuf, state,
             state_sem, load_sem, sib_s, sib_r, leaf_s, leaf_r, pay_s, pay_r,
             az_s, az_r, ay_s, ay_r, ax_s, ax_r, ac_s, ac_r, two_s, two_r):
    Z, NX, NY, H = dims
    K = Z // 2
    R = NX * NY
    n = lax.axis_index("node")
    r = lax.axis_index("rep")
    z, c = n // 2, n % 2
    x, y = r // NY, r % NY
    oc = 1 - c

    def zoff(off):
        return lax.rem(z + off + Z, Z)

    def dev(off, core):
        return (zoff(off) * 2 + core, r)

    master_copy = pltpu.make_async_copy(master_hbm, state, state_sem)
    master_copy.start()
    order = [K]
    for k in range(K - 1, 0, -1):
        order += [-k, k]
    order += [0]
    loads = {}

    def load(offs):
        for off in offs:
            d, i = zoff(off), off + K
            loads[off] = [
                pltpu.make_async_copy(g_hbm.at[d], gbuf.at[d], load_sem.at[0, i]),
                pltpu.make_async_copy(f_hbm.at[d], fbuf.at[d], load_sem.at[1, i]),
            ]
            for cp in loads[off]:
                cp.start()

    barrier = pltpu.get_barrier_semaphore()
    load(order[:1])
    for off in range(1, Z):
        pl.semaphore_signal(barrier, inc=1, device_id=dev(off, c), device_id_type=MESH)
    for off in (-1, 0, 1):
        pl.semaphore_signal(barrier, inc=1, device_id=dev(off, oc), device_id_type=MESH)
    load(order[1:3])

    def greet(i, carry):
        pl.semaphore_signal(barrier, inc=1, device_id=(n, lax.rem(r + i, R)), device_id_type=MESH)
        return carry

    lax.fori_loop(1, R, greet, 0)
    load(order[3:])

    def encode(off):
        d = zoff(off)
        for cp in loads[off]:
            cp.wait()

        xv = gbuf[d].astype(jnp.float32) + fbuf[d].astype(jnp.float32)
        dec = decoded_of(xv, 2.0**-12)
        dbuf[d] = dec.astype(jnp.bfloat16)
        ff_ref[d] = (xv - dec).astype(jnp.bfloat16)

    waits = []

    def remote(src, dst, ssem, rsem, to):
        cp = pltpu.make_async_remote_copy(
            src_ref=src, dst_ref=dst, send_sem=ssem, recv_sem=rsem, device_id=to, device_id_type=MESH
        )
        cp.start()
        waits.append(cp)
        return cp

    def level(dr, h):
        return K if dr == h else K - 1

    def sgn(dr):
        return -1 if dr == 0 else 1

    flying = {0: [], 1: []}

    def pace(dr):
        flying[dr] = []

    def send_leaf(dr, h):
        d = zoff(sgn(dr) * level(dr, h))
        pace(dr)
        for cc in range(2):
            flying[dr].append(remote(dbuf.at[d, cc, h], leaf.at[dr, h, c], leaf_s.at[dr, h, cc], leaf_r.at[dr, h, c],
                                     dev(sgn(dr), cc)))

    sib = {}

    def send_sib(off, h=None):
        d = zoff(off)
        if h is None:
            src, dst = dbuf.at[d, oc], sbuf.at[d]
        else:
            src, dst = dbuf.at[d, oc, h], sbuf.at[d, h]
        sib[off] = remote(src, dst, sib_s.at[off + K], sib_r.at[off + K], dev(0, oc))

    sib_seen = set()

    def wait_sib(off):
        if off not in sib_seen:
            sib_seen.add(off)
            sib[off].wait_recv()

    def received(dr, h, k):
        if k + 1 == level(dr, h):
            for src in range(2):
                pltpu.make_async_copy(leaf.at[dr, h, src], leaf.at[dr, h, src], leaf_r.at[dr, h, src]).wait()
            return leaf[dr, h, 0].astype(jnp.float32) + leaf[dr, h, 1].astype(jnp.float32)
        pltpu.make_async_copy(pay.at[dr, h, k], pay.at[dr, h, k], pay_r.at[dr, h, k]).wait()
        return pay[dr, h, k]

    def send_pay(dr, h, k):
        off = sgn(dr) * k
        d = zoff(off)
        wait_sib(off)
        acc = dbuf[d, c, h].astype(jnp.float32) + sbuf[d, h].astype(jnp.float32)
        out[dr, h, k] = acc + received(dr, h, k)
        pace(dr)
        flying[dr].append(remote(out.at[dr, h, k], pay.at[dr, h, k - 1], pay_s.at[dr, h, k],
                                 pay_r.at[dr, h, k - 1], dev(sgn(dr), c)))

    master_copy.wait()
    w_ref[z, c, x, y] = encode_master(state[...]).astype(jnp.bfloat16)
    encode(K)
    pl.semaphore_wait(barrier, (Z - 1) + 3 + (R - 1))
    gz = [remote(w_ref.at[z, c, x, y], w_ref.at[z, c, x, y], az_s.at[off], az_r.at[off], dev(off, c))
          for off in range(1, Z)]
    send_leaf(0, 0)
    send_leaf(1, 1)
    encode(-(K - 1))
    send_sib(-(K - 1), 0)
    encode(K - 1)
    send_sib(K - 1, 1)
    for k in range(K - 2, 0, -1):
        encode(-k)
        send_sib(-k)
        encode(k)
        send_sib(k)
    encode(0)
    send_sib(0)
    send_leaf(0, 1)
    send_leaf(1, 0)
    for cp in gz:
        cp.wait_recv()
    gy = [remote(w_ref.at[:, c, x, y], w_ref.at[:, c, x, y], ay_s.at[off], ay_r.at[off],
                 (n, x * NY + lax.rem(y + off, NY))) for off in range(1, NY)]

    def weights_x(stage):
        def to(off):
            return (n, lax.rem(x + off + NX, NX) * NY + y)

        def piece(off, part):
            return w_ref.at[part, c, lax.rem(x + off + NX, NX)]

        full = pl.ds(0, Z)
        if stage == 0:
            for cp in gy:
                cp.wait_recv()
            for i, off in enumerate((1, -1) if NX > 2 else (1,) if NX > 1 else ()):
                gx.append(remote(piece(0, full), piece(0, full), ax_s.at[i], ax_r.at[i], to(off)))
            to_sibling(piece(0, full), 0)
        if stage == 1:
            for i, off in enumerate((1, -1) if NX > 2 else (1,) if NX > 1 else ()):
                gx[i].wait_recv()
                if NX > 2:
                    half = piece(-off, pl.ds(i * Z // 2, Z // 2))
                    gx.append(remote(half, half, ax_s.at[2 + i], ax_r.at[2 + i], to(off)))
                to_sibling(piece(-off, full), 1 + i)
        if stage == 2 and NX > 2:
            for cp in gx[2:]:
                cp.wait_recv()
            to_sibling(piece(2, full), 3)

    def to_sibling(ref, i):
        gc.append(remote(ref, ref, ac_s.at[i], ac_r.at[i], dev(0, oc)))

    gx, gc = [], []
    for k in range(K - 1, 0, -1):
        for second in (True, False):
            for dr in range(2):
                h = dr if not second else 1 - dr
                if k < level(dr, h):
                    send_pay(dr, h, k)
            if k == 1 and second:
                weights_x(0)

    G = R // 2
    wait_sib(0)
    for h in (1, 0):
        part = dbuf[z, c, h].astype(jnp.float32) + sbuf[z, h].astype(jnp.float32)
        part = part + received(0, h, 0) + received(1, h, 0)
        two = decoded_of(part, 2.0**-15)
        ebuf[h * G:(h + 1) * G] = two.reshape(G, 8, LANES).astype(jnp.bfloat16)

        for j in range(NY):
            dy = NY // 2 + (1 - 2 * (j % 2)) * ((j + 1) // 2)
            for i in range(NX // 2):
                to = (h * NX // 2 + i) * NY + lax.rem(y + dy, NY)

                def send():
                    pltpu.make_async_remote_copy(
                        src_ref=ebuf.at[to], dst_ref=abuf.at[r], send_sem=two_s, recv_sem=two_r,
                        device_id=(n, to), device_id_type=MESH).start()

                if dy == 0:
                    pl.when(to != r)(send)
                else:
                    send()

    weights_x(1)
    abuf[r] = ebuf[r]
    rest = abuf.at[pl.ds(0, R - 1)]
    pltpu.make_async_copy(rest, rest, two_r).wait()
    total_ref[...] = jnp.sum(abuf[...].astype(jnp.float32), axis=0)
    weights_x(2)
    for cp in gc:
        cp.wait_recv()
    for cp in waits:
        cp.wait_send()
    pltpu.make_async_copy(rest, rest, two_s).wait()


def finish(devices, total_ref, master_ref, moment_ref, second_ref, ff_in, w_in,
           ff_out, mean_out, master_out, moment_out, second_out, w_out, small, sem):
    copies = [pltpu.make_async_copy(ff_in, ff_out, sem.at[4]), pltpu.make_async_copy(w_in, w_out, sem.at[5])]
    for cp in copies:
        cp.start()
    mean = total_ref[...] * (1.0 / devices)
    master = master_ref[...]
    moment = 0.9 * moment_ref[...] + 0.1 * mean
    second = 0.95 * second_ref[...] + 0.05 * mean * mean
    update = moment / 0.6513216 / (jnp.sqrt(second / 0.4012631) + 1e-08)
    small[0] = mean
    small[1] = master - 0.01 * (update + 0.1 * master)
    small[2] = moment
    small[3] = second
    for i, out in enumerate((mean_out, master_out, moment_out, second_out)):
        copies.append(pltpu.make_async_copy(small.at[i], out, sem.at[i]))
        copies[-1].start()
    for cp in copies:
        cp.wait()


def local(grads, feedback, master, moment, second):
    nodes, R = lax.axis_size("node"), lax.axis_size("rep")
    rows = grads.shape[2]
    Z = nodes // 2
    K = Z // 2
    NX = {32: 4, 4: 2}.get(R, 1)
    NY = R // NX
    H = rows // nodes // 2
    bf, f32 = jnp.bfloat16, jnp.float32
    blocks = (Z, 2, 2, H, LANES)
    wshape = (Z, 2, NX, NY, 8, LANES)
    hbm, vmem = pl.BlockSpec(memory_space=pltpu.HBM), pl.BlockSpec(memory_space=pltpu.VMEM)
    dma = pltpu.SemaphoreType.DMA
    ff, weights, total = pl.pallas_call(
        functools.partial(exchange, (Z, NX, NY, H)),
        out_shape=(
            jax.ShapeDtypeStruct(blocks, bf),
            jax.ShapeDtypeStruct(wshape, bf),
            jax.ShapeDtypeStruct((8, LANES), f32),
        ),
        in_specs=[hbm] * 3,
        out_specs=(vmem, vmem, vmem),
        scratch_shapes=[
            pltpu.VMEM(blocks, bf),
            pltpu.VMEM(blocks, bf),
            pltpu.VMEM(blocks, bf),
            pltpu.VMEM((Z, 2, H, LANES), bf),
            pltpu.VMEM((2, 2, 2, H, LANES), bf),
            pltpu.VMEM((2, 2, K, H, LANES), f32),
            pltpu.VMEM((2, 2, K, H, LANES), f32),
            pltpu.VMEM((R, 8, LANES), bf),
            pltpu.VMEM((R, 8, LANES), bf),
            pltpu.VMEM((8, LANES), f32),
            dma,
            dma((2, Z + 1)),
            dma((Z + 1,)), dma((Z + 1,)),
            dma((2, 2, 2)), dma((2, 2, 2)),
            dma((2, 2, K)), dma((2, 2, K)),
            dma((Z,)), dma((Z,)),
            dma((NY,)), dma((NY,)),
            dma((4,)), dma((4,)),
            dma((4,)), dma((4,)),
            dma, dma,
        ],
        compiler_params=pltpu.CompilerParams(
            collective_id=0, has_side_effects=True, vmem_limit_bytes=51 * 2**20 + 2**19
        ),
        cost_estimate=pl.CostEstimate(flops=20 * rows * LANES, bytes_accessed=10 * rows * LANES, transcendentals=0),
        name="exchange",
    )(grads.reshape(blocks), feedback.reshape(blocks), master)
    shard = jax.ShapeDtypeStruct((8, LANES), f32)
    ff, mean, new_master, new_moment, new_second, weights = pl.pallas_call(
        functools.partial(finish, nodes * R),
        out_shape=(jax.ShapeDtypeStruct(blocks, bf), shard, shard, shard, shard, jax.ShapeDtypeStruct(wshape, bf)),
        in_specs=[vmem] * 6,
        out_specs=(hbm,) * 6,
        scratch_shapes=[pltpu.VMEM((4, 8, LANES), f32), dma((6,))],
        compiler_params=pltpu.CompilerParams(vmem_limit_bytes=8 * 2**20),
        cost_estimate=pl.CostEstimate(flops=0, bytes_accessed=8 * rows * LANES, transcendentals=0),
        name="finish",
    )(total, master, moment, second, ff, weights)
    return (ff.reshape(grads.shape), mean, new_master, new_moment, new_second, weights.reshape(rows, LANES))


def solution(mesh):
    each, shard = P("node", "rep", None, None), P(("node", "rep"), None)
    return jax.shard_map(
        local,
        mesh=mesh,
        in_specs=(each, each, shard, shard, shard),
        out_specs=(each, shard, shard, shard, shard, P()),
        check_vma=False,
    )
```

time: 119 us -> 44.1 us (0.37)
  the two profiles are of different devices: /device:TPU:2 before, /device:TPU:1 now
where the time goes in v3:
time: 44.1 us; the launch traced here: 43.8 us
  Pallas kernels  41.8 us (95%)
  local copies, waits for them, and re-layouts  1.36 us (3%)
  between operations  0.67 us (2%)
    pallas_call x1, Pallas kernels, local(): pl.pallas_call(functools.partial(exchange, (Z, NX, NY, H)), out_shape=(ja...  40.5 us
    pallas_call x1, Pallas kernels, local(): pl.pallas_call(functools.partial(finish, nodes * R), out_shape=(jax.Shape...  1.37 us
    unnamed x6, local copies, waits for them, and re-layouts  1.36 us

profile of v3, /device:TPU:1, one launch (start us, length us, event | category | flops | bytes accessed | tf_op | source)
XLA Modules:
  0.0 43.8 jit_solution(5238841627304213780)
XLA Ops:
  0.6 0.0 copy-start
  0.6 0.7 %copy-done = f32[8,128]{1,0:T(8,128)S(1)} copy-done((f32[8,128]{1,0:T(8,128)S(1)}, f32[8,128]{1,0:T(8,128)}, u32[]{:S(2)}) %copy-start) | copy-done | bytes 4120
  1.3 0.0 copy-start.2
  1.3 40.5 %exchange.1 = (bf16[8,2,2,128,128]{4,3,2,1,0:T(8,128)(2,1)S(1)}, bf16[8,2,4,8,8,128]{5,4,3,2,1,0:T(8,128)(2,1)S(1)}, f32[8,128]{1,0:T(8,128)S(1)}) custom-call(bf16[8,2,2,128,128]{4,3,2,1,0:T(8,128)(2,1)} %bitcast.4, bf16[8,2,2,128,128]{4,3,2,1,0:T(8,128)(2,1)} %bitcast.5, f32[8,128]{1,0:T(8,128)S(1)} %copy-done), custom_call_target="tpu_custom_call" | custom-call | flops 10485760 | bytes 5242880 | tf_op jit(solution)/shard_map/exchange/pallas_call | solution.py:303
  41.8 0.0 copy-start.1
  41.8 0.0 copy-done.2
  41.8 0.7 %copy-done.1 = f32[8,128]{1,0:T(8,128)S(1)} copy-done((f32[8,128]{1,0:T(8,128)S(1)}, f32[8,128]{1,0:T(8,128)}, u32[]{:S(2)}) %copy-start.1) | copy-done | bytes 4120
  42.5 1.4 %finish.1 = (bf16[8,2,2,128,128]{4,3,2,1,0:T(8,128)(2,1)}, f32[8,128]{1,0:T(8,128)}, f32[8,128]{1,0:T(8,128)}, f32[8,128]{1,0:T(8,128)}, f32[8,128]{1,0:T(8,128)}, /*index=5*/bf16[8,2,4,8,8,128]{5,4,3,2,1,0:T(8,128)(2,1)}) custom-call(f32[8,128]{1,0:T(8,128)S(1)} %get-tuple-element.15.total_ref, f32[8,128]{1,0:T(8,128)S(1)} %copy-done, ...), custom_call_target="tpu_custom_call" | custom-call | bytes 4194304 | tf_op jit(solution)/shard_map/finish/pallas_call | solution.py:341
Async XLA Ops:
  0.6 0.7 %copy-start = (f32[8,128]{1,0:T(8,128)S(1)}, f32[8,128]{1,0:T(8,128)}, u32[]{:S(2)}) copy-start(f32[8,128]{1,0:T(8,128)} %master_ref.1) | copy-start | bytes 12292
  1.3 40.5 %copy-start.2 = (f32[8,128]{1,0:T(8,128)S(1)}, f32[8,128]{1,0:T(8,128)}, u32[]{:S(2)}) copy-start(f32[8,128]{1,0:T(8,128)} %second_ref.1) | copy-start | bytes 12292
  41.8 0.7 %copy-start.1 = (f32[8,128]{1,0:T(8,128)S(1)}, f32[8,128]{1,0:T(8,128)}, u32[]{:S(2)}) copy-start(f32[8,128]{1,0:T(8,128)} %moment_ref.1) | copy-start | bytes 12292

commit v4 on v3

--- a/solution.py
+++ b/solution.py
@@ -25,6 +25,10 @@
     bound = scale * 0.875
     rounded = ((values + nudge) + magic) - magic
     return jnp.minimum(jnp.maximum(rounded, -bound), bound)
+
+
+def farthest_first(size):
+    return sorted(range(1, size), key=lambda off: -min(off, size - off))
 
 
 def encode_master(values):
@@ -40,9 +44,9 @@
     return scale * code * (1.0 / 128.0)
 
 
-def exchange(dims, g_hbm, f_hbm, master_hbm, ff_ref, w_ref, total_ref,
-             gbuf, fbuf, dbuf, sbuf, leaf, pay, out, ebuf, abuf, state,
-             state_sem, load_sem, sib_s, sib_r, leaf_s, leaf_r, pay_s, pay_r,
+def exchange(dims, g_hbm, f_hbm, master_ref, ff_ref, w_ref, total_ref,
+             gbuf, fbuf, dbuf, sbuf, leaf, pay, out, ebuf, abuf,
+             load_sem, sib_s, sib_r, leaf_s, leaf_r, pay_s, pay_r,
              az_s, az_r, ay_s, ay_r, ax_s, ax_r, ac_s, ac_r, two_s, two_r):
     Z, NX, NY, H = dims
     K = Z // 2
@@ -59,8 +63,6 @@
     def dev(off, core):
         return (zoff(off) * 2 + core, r)
 
-    master_copy = pltpu.make_async_copy(master_hbm, state, state_sem)
-    master_copy.start()
     order = [K]
     for k in range(K - 1, 0, -1):
         order += [-k, k]
@@ -83,14 +85,12 @@
         pl.semaphore_signal(barrier, inc=1, device_id=dev(off, c), device_id_type=MESH)
     for off in (-1, 0, 1):
         pl.semaphore_signal(barrier, inc=1, device_id=dev(off, oc), device_id_type=MESH)
-    load(order[1:3])
-
-    def greet(i, carry):
-        pl.semaphore_signal(barrier, inc=1, device_id=(n, lax.rem(r + i, R)), device_id_type=MESH)
-        return carry
-
-    lax.fori_loop(1, R, greet, 0)
-    load(order[3:])
+    for dx in range(NX):
+        for dy in range(NY):
+            if dx or dy:
+                pl.semaphore_signal(barrier, inc=1, device_id_type=MESH,
+                                    device_id=(n, lax.rem(x + dx, NX) * NY + lax.rem(y + dy, NY)))
+    load(order[1:])
 
     def encode(off):
         d = zoff(off)
@@ -118,17 +118,11 @@
     def sgn(dr):
         return -1 if dr == 0 else 1
 
-    flying = {0: [], 1: []}
-
-    def pace(dr):
-        flying[dr] = []
-
     def send_leaf(dr, h):
         d = zoff(sgn(dr) * level(dr, h))
-        pace(dr)
         for cc in range(2):
-            flying[dr].append(remote(dbuf.at[d, cc, h], leaf.at[dr, h, c], leaf_s.at[dr, h, cc], leaf_r.at[dr, h, c],
-                                     dev(sgn(dr), cc)))
+            remote(dbuf.at[d, cc, h], leaf.at[dr, h, c], leaf_s.at[dr, h, cc], leaf_r.at[dr, h, c],
+                   dev(sgn(dr), cc))
 
     sib = {}
 
@@ -161,35 +155,29 @@
         wait_sib(off)
         acc = dbuf[d, c, h].astype(jnp.float32) + sbuf[d, h].astype(jnp.float32)
         out[dr, h, k] = acc + received(dr, h, k)
-        pace(dr)
-        flying[dr].append(remote(out.at[dr, h, k], pay.at[dr, h, k - 1], pay_s.at[dr, h, k],
-                                 pay_r.at[dr, h, k - 1], dev(sgn(dr), c)))
-
-    master_copy.wait()
-    w_ref[z, c, x, y] = encode_master(state[...]).astype(jnp.bfloat16)
-    encode(K)
+        remote(out.at[dr, h, k], pay.at[dr, h, k - 1], pay_s.at[dr, h, k], pay_r.at[dr, h, k - 1],
+               dev(sgn(dr), c))
+
+    w_ref[z, c, x, y] = encode_master(master_ref[...]).astype(jnp.bfloat16)
+    for off in order:
+        encode(off)
     pl.semaphore_wait(barrier, (Z - 1) + 3 + (R - 1))
     gz = [remote(w_ref.at[z, c, x, y], w_ref.at[z, c, x, y], az_s.at[off], az_r.at[off], dev(off, c))
-          for off in range(1, Z)]
+          for off in farthest_first(Z)]
     send_leaf(0, 0)
     send_leaf(1, 1)
-    encode(-(K - 1))
     send_sib(-(K - 1), 0)
-    encode(K - 1)
     send_sib(K - 1, 1)
-    for k in range(K - 2, 0, -1):
-        encode(-k)
-        send_sib(-k)
-        encode(k)
-        send_sib(k)
-    encode(0)
-    send_sib(0)
     send_leaf(0, 1)
     send_leaf(1, 0)
+    for k in range(K - 2, 0, -1):
+        send_sib(-k)
+        send_sib(k)
+    send_sib(0)
     for cp in gz:
         cp.wait_recv()
     gy = [remote(w_ref.at[:, c, x, y], w_ref.at[:, c, x, y], ay_s.at[off], ay_r.at[off],
-                 (n, x * NY + lax.rem(y + off, NY))) for off in range(1, NY)]
+                 (n, x * NY + lax.rem(y + off, NY))) for off in farthest_first(NY)]
 
     def weights_x(stage):
         def to(off):
@@ -307,7 +295,7 @@
             jax.ShapeDtypeStruct(wshape, bf),
             jax.ShapeDtypeStruct((8, LANES), f32),
         ),
-        in_specs=[hbm] * 3,
+        in_specs=[hbm, hbm, vmem],
         out_specs=(vmem, vmem, vmem),
         scratch_shapes=[
             pltpu.VMEM(blocks, bf),
@@ -319,8 +307,6 @@
             pltpu.VMEM((2, 2, K, H, LANES), f32),
             pltpu.VMEM((R, 8, LANES), bf),
             pltpu.VMEM((R, 8, LANES), bf),
-            pltpu.VMEM((8, LANES), f32),
-            dma,
             dma((2, Z + 1)),
             dma((Z + 1,)), dma((Z + 1,)),
             dma((2, 2, 2)), dma((2, 2, 2)),

time: 44.1 us -> 44 us (level)
  no operation moved by 1% of the time
where the time goes in v4:
time: 44 us; the launch traced here: 43.8 us
  Pallas kernels  41.7 us (95%)
  local copies, waits for them, and re-layouts  1.36 us (3%)
  between operations  0.67 us (2%)
    pallas_call x1, Pallas kernels, local(): pl.pallas_call(functools.partial(exchange, (Z, NX, NY, H)), out_shape=(ja...  40.4 us
    pallas_call x1, Pallas kernels, local(): pl.pallas_call(functools.partial(finish, nodes * R), out_shape=(jax.Shape...  1.37 us
    unnamed x6, local copies, waits for them, and re-layouts  1.36 us

profile of v4, /device:TPU:1, one launch (start us, length us, event | category | flops | bytes accessed | tf_op | source)
XLA Modules:
  0.0 43.8 jit_solution(7224665219123720017)
XLA Ops:
  0.6 0.0 copy-start
  0.6 0.7 %copy-done = f32[8,128]{1,0:T(8,128)S(1)} copy-done((f32[8,128]{1,0:T(8,128)S(1)}, f32[8,128]{1,0:T(8,128)}, u32[]{:S(2)}) %copy-start) | copy-done | bytes 4120
  1.3 0.0 copy-start.2
  1.3 40.4 %exchange.1 = (bf16[8,2,2,128,128]{4,3,2,1,0:T(8,128)(2,1)S(1)}, bf16[8,2,4,8,8,128]{5,4,3,2,1,0:T(8,128)(2,1)S(1)}, f32[8,128]{1,0:T(8,128)S(1)}) custom-call(bf16[8,2,2,128,128]{4,3,2,1,0:T(8,128)(2,1)} %bitcast.4, bf16[8,2,2,128,128]{4,3,2,1,0:T(8,128)(2,1)} %bitcast.5, f32[8,128]{1,0:T(8,128)S(1)} %copy-done), custom_call_target="tpu_custom_call" | custom-call | flops 10485760 | bytes 5242880 | tf_op jit(solution)/shard_map/exchange/pallas_call | solution.py:291
  41.7 0.0 copy-start.1
  41.7 0.0 copy-done.2
  41.7 0.7 %copy-done.1 = f32[8,128]{1,0:T(8,128)S(1)} copy-done((f32[8,128]{1,0:T(8,128)S(1)}, f32[8,128]{1,0:T(8,128)}, u32[]{:S(2)}) %copy-start.1) | copy-done | bytes 4120
  42.4 1.4 %finish.1 = (bf16[8,2,2,128,128]{4,3,2,1,0:T(8,128)(2,1)}, f32[8,128]{1,0:T(8,128)}, f32[8,128]{1,0:T(8,128)}, f32[8,128]{1,0:T(8,128)}, f32[8,128]{1,0:T(8,128)}, /*index=5*/bf16[8,2,4,8,8,128]{5,4,3,2,1,0:T(8,128)(2,1)}) custom-call(f32[8,128]{1,0:T(8,128)S(1)} %get-tuple-element.15.total_ref, f32[8,128]{1,0:T(8,128)S(1)} %copy-done, ...), custom_call_target="tpu_custom_call" | custom-call | bytes 4194304 | tf_op jit(solution)/shard_map/finish/pallas_call | solution.py:327
Async XLA Ops:
  0.6 0.7 %copy-start = (f32[8,128]{1,0:T(8,128)S(1)}, f32[8,128]{1,0:T(8,128)}, u32[]{:S(2)}) copy-start(f32[8,128]{1,0:T(8,128)} %master_ref.3) | copy-start | bytes 12292
  1.3 40.4 %copy-start.2 = (f32[8,128]{1,0:T(8,128)S(1)}, f32[8,128]{1,0:T(8,128)}, u32[]{:S(2)}) copy-start(f32[8,128]{1,0:T(8,128)} %second_ref.1) | copy-start | bytes 12292
  41.7 0.7 %copy-start.1 = (f32[8,128]{1,0:T(8,128)S(1)}, f32[8,128]{1,0:T(8,128)}, u32[]{:S(2)}) copy-start(f32[8,128]{1,0:T(8,128)} %moment_ref.1) | copy-start | bytes 12292

commit v5 on v4

--- a/solution.py
+++ b/solution.py
@@ -218,28 +218,28 @@
             if k == 1 and second:
                 weights_x(0)
 
-    G = R // 2
     wait_sib(0)
-    for h in (1, 0):
+    parts = []
+    for h in range(2):
         part = dbuf[z, c, h].astype(jnp.float32) + sbuf[z, h].astype(jnp.float32)
         part = part + received(0, h, 0) + received(1, h, 0)
-        two = decoded_of(part, 2.0**-15)
-        ebuf[h * G:(h + 1) * G] = two.reshape(G, 8, LANES).astype(jnp.bfloat16)
-
-        for j in range(NY):
-            dy = NY // 2 + (1 - 2 * (j % 2)) * ((j + 1) // 2)
-            for i in range(NX // 2):
-                to = (h * NX // 2 + i) * NY + lax.rem(y + dy, NY)
-
-                def send():
-                    pltpu.make_async_remote_copy(
-                        src_ref=ebuf.at[to], dst_ref=abuf.at[r], send_sem=two_s, recv_sem=two_r,
-                        device_id=(n, to), device_id_type=MESH).start()
-
-                if dy == 0:
-                    pl.when(to != r)(send)
-                else:
-                    send()
+        parts.append(part)
+    two = decoded_of(jnp.concatenate(parts, axis=0), 2.0**-15)
+    ebuf[...] = two.reshape(R, 8, LANES).astype(jnp.bfloat16)
+    for j in range(NY):
+        dy = NY // 2 + (1 - 2 * (j % 2)) * ((j + 1) // 2)
+        for i in range(NX):
+            to = i * NY + lax.rem(y + dy, NY)
+
+            def send():
+                pltpu.make_async_remote_copy(
+                    src_ref=ebuf.at[to], dst_ref=abuf.at[r], send_sem=two_s, recv_sem=two_r,
+                    device_id=(n, to), device_id_type=MESH).start()
+
+            if dy == 0:
+                pl.when(to != r)(send)
+            else:
+                send()
 
     weights_x(1)
     abuf[r] = ebuf[r]

time: 44 us -> 43.8 us (level)
  no operation moved by 1% of the time
where the time goes in v5:
time: 43.8 us; the launch traced here: 43.6 us
  Pallas kernels  41.5 us (95%)
  local copies, waits for them, and re-layouts  1.36 us (3%)
  between operations  0.67 us (2%)
    pallas_call x1, Pallas kernels, local(): pl.pallas_call(functools.partial(exchange, (Z, NX, NY, H)), out_shape=(ja...  40.2 us
    pallas_call x1, Pallas kernels, local(): pl.pallas_call(functools.partial(finish, nodes * R), out_shape=(jax.Shape...  1.37 us
    unnamed x6, local copies, waits for them, and re-layouts  1.36 us

profile of v5, /device:TPU:1, one launch (start us, length us, event | category | flops | bytes accessed | tf_op | source)
XLA Modules:
  0.0 43.6 jit_solution(8748892396457445927)
XLA Ops:
  0.6 0.0 copy-start
  0.6 0.7 %copy-done = f32[8,128]{1,0:T(8,128)S(1)} copy-done((f32[8,128]{1,0:T(8,128)S(1)}, f32[8,128]{1,0:T(8,128)}, u32[]{:S(2)}) %copy-start) | copy-done | bytes 4120
  1.3 0.0 copy-start.2
  1.3 40.2 %exchange.1 = (bf16[8,2,2,128,128]{4,3,2,1,0:T(8,128)(2,1)S(1)}, bf16[8,2,4,8,8,128]{5,4,3,2,1,0:T(8,128)(2,1)S(1)}, f32[8,128]{1,0:T(8,128)S(1)}) custom-call(bf16[8,2,2,128,128]{4,3,2,1,0:T(8,128)(2,1)} %bitcast.4, bf16[8,2,2,128,128]{4,3,2,1,0:T(8,128)(2,1)} %bitcast.5, f32[8,128]{1,0:T(8,128)S(1)} %copy-done), custom_call_target="tpu_custom_call" | custom-call | flops 10485760 | bytes 5242880 | tf_op jit(solution)/shard_map/exchange/pallas_call | solution.py:291
  41.5 0.0 copy-start.1
  41.5 0.0 copy-done.2
  41.5 0.7 %copy-done.1 = f32[8,128]{1,0:T(8,128)S(1)} copy-done((f32[8,128]{1,0:T(8,128)S(1)}, f32[8,128]{1,0:T(8,128)}, u32[]{:S(2)}) %copy-start.1) | copy-done | bytes 4120
  42.2 1.4 %finish.1 = (bf16[8,2,2,128,128]{4,3,2,1,0:T(8,128)(2,1)}, f32[8,128]{1,0:T(8,128)}, f32[8,128]{1,0:T(8,128)}, f32[8,128]{1,0:T(8,128)}, f32[8,128]{1,0:T(8,128)}, /*index=5*/bf16[8,2,4,8,8,128]{5,4,3,2,1,0:T(8,128)(2,1)}) custom-call(f32[8,128]{1,0:T(8,128)S(1)} %get-tuple-element.15.total_ref, f32[8,128]{1,0:T(8,128)S(1)} %copy-done, ...), custom_call_target="tpu_custom_call" | custom-call | bytes 4194304 | tf_op jit(solution)/shard_map/finish/pallas_call | solution.py:327
Async XLA Ops:
  0.6 0.7 %copy-start = (f32[8,128]{1,0:T(8,128)S(1)}, f32[8,128]{1,0:T(8,128)}, u32[]{:S(2)}) copy-start(f32[8,128]{1,0:T(8,128)} %master_ref.3) | copy-start | bytes 12292
  1.3 40.2 %copy-start.2 = (f32[8,128]{1,0:T(8,128)S(1)}, f32[8,128]{1,0:T(8,128)}, u32[]{:S(2)}) copy-start(f32[8,128]{1,0:T(8,128)} %second_ref.1) | copy-start | bytes 12292
  41.5 0.7 %copy-start.1 = (f32[8,128]{1,0:T(8,128)S(1)}, f32[8,128]{1,0:T(8,128)}, u32[]{:S(2)}) copy-start(f32[8,128]{1,0:T(8,128)} %moment_ref.1) | copy-start | bytes 12292
